TPU v7x, 256 devices: a whole 4x4x8 slice. The times are simulated.
256 devices in a mesh: section: 32 (over z, x_lo, core), tp: 8 (over y, x_hi).
Axes of the slice: x: 4 (x_hi: 2, x_lo: 2; x = x_hi * 2 + x_lo), y: 4, z: 8, core: 2. Of those that a mesh axis runs over, the one named last changes fastest.
Arguments:
- weights: bfloat16 [32, 1024, 8192], P('section', 'tp'), may hold values from -0.5 to 0.5
- mirror_weights: bfloat16 [32, 1024, 8192], P('section', 'tp'), may hold values from -0.5 to 0.5
- acts_down: bfloat16 [32, 256, 8192], P('section', None, 'tp'), may hold values from -8 to 8
- cot_down: bfloat16 [32, 256, 8192], P('section', None, 'tp'), may hold values from -6 to 6
- key_cotangent_lower: bfloat16 [32, 256, 1024], P('section', None, 'tp'), may hold values from -6 to 6
- acts_up: bfloat16 [32, 256, 8192], P('section', None, 'tp'), may hold values from -8 to 8
- cot_up: bfloat16 [32, 256, 8192], P('section', None, 'tp'), may hold values from -6 to 6
- key_cot_up: bfloat16 [32, 256, 1024], P('section', None, 'tp'), may hold values from -6 to 6
Outputs:
- weight_grad: bfloat16 [32, 1024, 8192], P('section', 'tp')
- grad_down: bfloat16 [32, 256, 8192], P('section', None, 'tp')
- grad_up: bfloat16 [32, 256, 8192], P('section', None, 'tp')
All inputs are finite; a program needn't handle non-finite values.
Results may differ from a plain program's by a relative error of at most 0.014.
Values may be sent and summed in bfloat16 or wider, within the bound.
A program may use at most 192 MiB of HBM per device.

v0:
```python
import jax
import jax.numpy as jnp
from jax import lax
from jax.sharding import PartitionSpec as P

epsilon = 1e-05


def from_partner(value, axis, apart):
    mask = 2**apart
    pairs = [(source, source ^ mask) for source in range(lax.axis_size(axis))]
    return lax.ppermute(value, axis, pairs)


def from_behind(shard, axis, by):
    devices = lax.axis_size(axis)
    pairs = [(i, i + by) for i in range(devices) if 0 <= i + by < devices]
    return lax.ppermute(shard, axis, pairs)


def key_product(cot_rows, normed_rows):
    return lax.dot_general(
        cot_rows, normed_rows, (((0,), (0,)), ((), ())), preferred_element_type=jnp.float32
    )


def per_device(
    weights, mirror_weights, acts_down, cot_down, key_cotangent_lower, acts_up, cot_up, key_cot_up
):
    weight_own = weights[0]
    weight_far = mirror_weights[0]
    near_x = acts_down[0]
    near_c = cot_down[0]
    near_g = key_cotangent_lower[0]
    far_x = acts_up[0]
    far_c = cot_up[0]
    far_g = key_cot_up[0]
    row_count = near_x.shape[0]
    section_bits = lax.axis_size("section").bit_length() - 1
    bit_list = list(range(section_bits))
    rows_x = jnp.concatenate([near_x, far_x], axis=0)
    full_x = lax.all_gather(rows_x, "tp", axis=1, tiled=True)
    inputs = full_x.astype(jnp.float32)
    inv_rms = lax.rsqrt(jnp.mean(inputs * inputs, axis=1, keepdims=True) + epsilon)
    normed = inputs * inv_rms
    normed_half = normed.astype(jnp.bfloat16)
    key_near = key_product(near_g, normed_half[:row_count])
    sent = key_product(far_g, normed_half[row_count : 2 * row_count]).astype(jnp.bfloat16)
    for each_bit in bit_list:
        sent = from_partner(sent, "section", each_bit)
    weight_grad = key_near + sent.astype(jnp.float32)
    part_near = jnp.dot(near_g, weight_own, preferred_element_type=jnp.float32)
    distant_portion = jnp.dot(far_g, weight_far, preferred_element_type=jnp.float32)
    partial_value_term = jnp.concatenate([part_near, distant_portion], axis=0)
    shard_width = near_x.shape[1]
    offset = lax.axis_index("tp") * shard_width
    own_normed = lax.dynamic_slice_in_dim(normed, offset, shard_width, 1)
    hidden_grad = lax.psum_scatter(
        partial_value_term.astype(jnp.bfloat16), "tp", scatter_dimension=1, tiled=True
    ).astype(jnp.float32)
    local_dots = jnp.sum(hidden_grad * own_normed, axis=1, keepdims=True)
    row_dots = lax.psum(local_dots, "tp") / full_x.shape[1]
    rows_c = jnp.concatenate([near_c, far_c], axis=0)
    result = (rows_c.astype(jnp.float32) + inv_rms * (hidden_grad - own_normed * row_dots)).astype(
        jnp.bfloat16
    )
    grad_down = from_behind(result[:row_count], "section", -1)
    grad_up = from_behind(result[row_count:], "section", 1)
    return (weight_grad.astype(jnp.bfloat16)[None], grad_down[None], grad_up[None])


def solution(mesh):
    in_specs = (
        P("section", "tp", None),
        P("section", "tp", None),
        P("section", None, "tp"),
        P("section", None, "tp"),
        P("section", None, "tp"),
        P("section", None, "tp"),
        P("section", None, "tp"),
        P("section", None, "tp"),
    )
    out_specs = (P("section", "tp", None), P("section", None, "tp"), P("section", None, "tp"))
    return jax.shard_map(
        per_device, mesh=mesh, in_specs=in_specs, out_specs=out_specs, check_vma=False
    )
```

profile of v0, /device:TPU:1, one launch (start us, length us, event | category | flops | bytes accessed | tf_op | source)
XLA Modules:
  0.0 473.1 jit_solution(5948506858705521863)
XLA Ops:
  7.2 0.0 copy-start
  7.2 0.0 all-gather.2.cloned.1.call-start
  7.2 2.4 pad_maximum_fusion.1
  9.6 0.0 copy-start.8
  9.6 0.0 all-gather.2.cloned.1.call-update
  9.6 0.0 reduce-scatter.2.cloned.1.call-start
  9.7 0.0 copy-done
  9.7 0.0 copy-start.4
  9.7 4.2 convolution_convert_fusion.1
  13.9 0.0 copy-done.8
  13.9 0.0 copy-done.4
  13.9 3.2 convolution_convert_fusion
  17.1 7.7 %pad_maximum_fusion = bf16[512,8192]{1,0:T(8,128)(2,1)} fusion(bf16[256,8192]{1,0:T(8,128)(2,1)} %convolution_convert_fusion, bf16[256,8192]{1,0:T(8,128)(2,1)} %convolution_convert_fusion.1), kind=kLoop, calls=%fused_computation.8 | loop fusion | flops 16777216 | bytes 16777216 | tf_op jit(solution)/shard_map/concatenate | solution.py:54
  24.7 0.0 reduce-scatter.2.cloned.1.call-update
  24.8 102.0 %all-gather.2.cloned.1.call-done = bf16[512,8192]{1,0:T(8,128)(2,1)} async-done(((bf16[512,1024]{1,0:T(8,128)(2,1)}), bf16[512,8192]{1,0:T(8,128)(2,1)}) %all-gather.2.cloned.1.call-update) | async-done | bytes 8388624 | tf_op jit(solution)/shard_map/all_gather | solution.py:42
  126.8 5.3 %fusion = f32[512]{0:T(512)S(1)} fusion(bf16[512,8192]{1,0:T(8,128)(2,1)} %all-gather.2.cloned.1.call-done), kind=kLoop, calls=%fused_computation.2 | loop fusion | flops 12582400 | bytes 8390656 | tf_op jit(solution)/shard_map/reduce_sum | solution.py:44
  132.0 0.5 copy-done.2
  132.5 6.5 %convert_multiply_fusion = (f32[512,8192]{1,0:T(8,128)}, bf16[512,8192]{1,0:T(8,128)(2,1)S(1)}) fusion(bf16[512,8192]{1,0:T(8,128)(2,1)S(1)} %copy-done.2, f32[512]{0:T(512)S(1)} %add_rsqrt_fusion), kind=kLoop, calls=%fused_computation | loop fusion | flops 12582912 | bytes 33556480 | tf_op jit(solution)/shard_map/mul | solution.py:45
  139.0 1.3 fusion.1
  140.3 2.6 copy-done.3
  142.9 1.1 collective-permute-start
  144.0 3.8 collective-permute-done
  147.8 0.3 collective-permute-start.1
  148.1 72.8 %collective-permute-done.1 = bf16[128,8192]{0,1:T(8,128)(2,1)S(1)} collective-permute-done((bf16[128,8192]{0,1:T(8,128)(2,1)S(1)}, bf16[128,8192]{0,1:T(8,128)(2,1)S(1)}, u32[]{:S(2)}, u32[]{:S(2)}) %collective-permute-start.1) | collective-permute-done | bytes 2097184 | tf_op jit(solution)/shard_map/ppermute | solution.py:12
  220.8 1.3 collective-permute-start.2
  222.1 45.1 %collective-permute-done.2 = bf16[128,8192]{0,1:T(8,128)(2,1)S(1)} collective-permute-done((bf16[128,8192]{0,1:T(8,128)(2,1)S(1)}, bf16[128,8192]{0,1:T(8,128)(2,1)S(1)}, u32[]{:S(2)}, u32[]{:S(2)}) %collective-permute-start.2) | collective-permute-done | bytes 2097184 | tf_op jit(solution)/shard_map/ppermute | solution.py:12
  267.2 2.3 collective-permute-start.3
  269.5 90.2 %collective-permute-done.3 = bf16[128,8192]{0,1:T(8,128)(2,1)} collective-permute-done((bf16[128,8192]{0,1:T(8,128)(2,1)S(1)}, bf16[128,8192]{0,1:T(8,128)(2,1)}, u32[]{:S(2)}, u32[]{:S(2)}) %collective-permute-start.3) | collective-permute-done | bytes 2097184 | tf_op jit(solution)/shard_map/ppermute | solution.py:12
  359.7 6.4 %collective-permute-start.4 = (bf16[128,8192]{0,1:T(8,128)(2,1)}, bf16[128,8192]{0,1:T(8,128)(2,1)}, u32[]{:S(2)}, u32[]{:S(2)}) collective-permute-start(bf16[128,8192]{0,1:T(8,128)(2,1)} %collective-permute-done.3), channel_id=1, source_target_pairs={{0,128},{8,136},{16,144},{24,152},{32,160},{40,168},{48,176},{56,1... | collective-permute-start | bytes 6291464 | tf_op jit(solution)/shard_map/ppermute | solution.py:12
  366.1 2.2 fusion.4
  368.3 0.0 copy-start.7
  368.3 20.3 %psum.7 = f32[512,1]{0,1:T(1,128)S(1)} all-reduce(f32[512,1]{0,1:T(1,128)S(1)} %bitcast.37), channel_id=1, replica_groups=mesh['section'=32,'tp'=8] {'tp'}, use_global_device_ids=true, to_apply=%region_3.0 | all-reduce | flops 512 | bytes 4096 | tf_op jit(solution)/shard_map/psum | solution.py:62
  388.6 0.0 copy-done.5
  388.6 0.0 copy-done.6
  388.6 2.4 fusion.7
  391.1 0.1 fusion.16
  391.1 5.7 %collective-permute-start.6 = (bf16[256,1024]{1,0:T(8,128)(2,1)S(1)}, bf16[256,1024]{1,0:T(8,128)(2,1)S(1)}, u32[]{:S(2)}, u32[]{:S(2)}) collective-permute-start(bf16[256,1024]{1,0:T(8,128)(2,1)S(1)} %get-tuple-element.11), channel_id=1, source_target_pairs={{0,8},{8,16},{16,24},{24,32},{32,40},{40,48},{48,56},{56,64},{64,7... | collective-permute-start | bytes 1572872 | tf_op jit(solution)/shard_map/ppermute | solution.py:18
  396.9 1.9 collective-permute-start.5
  398.8 0.0 copy-done.7
  398.8 3.5 convolution_bitcast_fusion
  402.3 0.7 collective-permute-done.6
  403.0 4.8 %collective-permute-done.5 = bf16[256,1024]{1,0:T(8,128)(2,1)S(1)} collective-permute-done((bf16[256,1024]{1,0:T(8,128)(2,1)S(1)}, bf16[256,1024]{1,0:T(8,128)(2,1)S(1)}, u32[]{:S(2)}, u32[]{:S(2)}) %collective-permute-start.5) | collective-permute-done | bytes 524320 | tf_op jit(solution)/shard_map/ppermute | solution.py:18
  407.8 49.2 %collective-permute-done.4 = bf16[128,8192]{0,1:T(8,128)(2,1)} collective-permute-done((bf16[128,8192]{0,1:T(8,128)(2,1)}, bf16[128,8192]{0,1:T(8,128)(2,1)}, u32[]{:S(2)}, u32[]{:S(2)}) %collective-permute-start.4) | collective-permute-done | bytes 2097184 | tf_op jit(solution)/shard_map/ppermute | solution.py:12
  457.0 3.6 fusion.8
  460.6 4.1 copy.12
  464.7 0.8 copy.15
  465.5 0.8 copy.16
  466.3 0.0 copy-done.1
  (8 shorter events, 0.0 us)
Async XLA Ops:
  7.2 2.5 copy-start
  7.2 119.6 %all-gather.2.cloned.1.call-start = ((), (), s32[]{:S(2)}) async-start(), calls=%async_computation.1 | async-start | bytes 9437184 | tf_op jit(solution)/shard_map/all_gather | solution.py:42
  9.6 4.3 copy-start.8
  9.6 356.5 %reduce-scatter.2.cloned.1.call-start = ((), (), s32[]{:S(2)}) async-start(), calls=%async_computation.2 | async-start | bytes 9437184 | tf_op jit(solution)/shard_map/reduce_scatter | solution.py:58
  9.7 4.2 copy-start.4
  126.8 5.8 %copy-start.2 = (bf16[512,8192]{1,0:T(8,128)(2,1)S(1)}, bf16[512,8192]{1,0:T(8,128)(2,1)}, u32[]{:S(2)}) copy-start(bf16[512,8192]{1,0:T(8,128)(2,1)} %all-gather.2.cloned.1.call-done) | copy-start | bytes 25165828
  139.0 3.9 copy-start.3
  139.0 249.6 %copy-start.5 = (bf16[1,256,1024]{2,1,0:T(8,128)(2,1)S(1)}, bf16[1,256,1024]{2,1,0:T(8,128)(2,1)}, u32[]{:S(2)}) copy-start(bf16[1,256,1024]{2,1,0:T(8,128)(2,1)} %param.14) | copy-start | bytes 1572868
  139.0 249.6 %copy-start.6 = (bf16[1,256,1024]{2,1,0:T(8,128)(2,1)S(1)}, bf16[1,256,1024]{2,1,0:T(8,128)(2,1)}, u32[]{:S(2)}) copy-start(bf16[1,256,1024]{2,1,0:T(8,128)(2,1)} %param.11) | copy-start | bytes 1572868
  142.9 4.9 %collective-permute-start = (bf16[128,8192]{0,1:T(8,128)(2,1)S(1)}, bf16[128,8192]{0,1:T(8,128)(2,1)S(1)}, u32[]{:S(2)}, u32[]{:S(2)}) collective-permute-start(bf16[128,8192]{0,1:T(8,128)(2,1)S(1)} %fusion.1), channel_id=1, source_target_pairs={{0,8},{8,0},{16,24},{24,16},{32,40},{40,32},{48,56},{56,48},{64,72... | collective-permute-start | bytes 6291464 | tf_op jit(solution)/shard_map/ppermute | solution.py:12
  147.8 73.1 %collective-permute-start.1 = (bf16[128,8192]{0,1:T(8,128)(2,1)S(1)}, bf16[128,8192]{0,1:T(8,128)(2,1)S(1)}, u32[]{:S(2)}, u32[]{:S(2)}) collective-permute-start(bf16[128,8192]{0,1:T(8,128)(2,1)S(1)} %collective-permute-done), channel_id=1, source_target_pairs={{0,16},{8,24},{16,0},{24,8},{32,48},{40,56},{48,32},{56,40},{64,80... | collective-permute-start | bytes 6291464 | tf_op jit(solution)/shard_map/ppermute | solution.py:12
  220.8 46.4 %collective-permute-start.2 = (bf16[128,8192]{0,1:T(8,128)(2,1)S(1)}, bf16[128,8192]{0,1:T(8,128)(2,1)S(1)}, u32[]{:S(2)}, u32[]{:S(2)}) collective-permute-start(bf16[128,8192]{0,1:T(8,128)(2,1)S(1)} %collective-permute-done.1), channel_id=1, source_target_pairs={{0,32},{8,40},{16,48},{24,56},{32,0},{40,8},{48,16},{56,24},{64,96... | collective-permute-start | bytes 6291464 | tf_op jit(solution)/shard_map/ppermute | solution.py:12
  267.2 92.4 %collective-permute-start.3 = (bf16[128,8192]{0,1:T(8,128)(2,1)S(1)}, bf16[128,8192]{0,1:T(8,128)(2,1)}, u32[]{:S(2)}, u32[]{:S(2)}) collective-permute-start(bf16[128,8192]{0,1:T(8,128)(2,1)S(1)} %collective-permute-done.2), channel_id=1, source_target_pairs={{0,64},{8,72},{16,80},{24,88},{32,96},{40,104},{48,112},{56,120},{... | collective-permute-start | bytes 6291464 | tf_op jit(solution)/shard_map/ppermute | solution.py:12
  359.7 97.3 %collective-permute-start.4 = (bf16[128,8192]{0,1:T(8,128)(2,1)}, bf16[128,8192]{0,1:T(8,128)(2,1)}, u32[]{:S(2)}, u32[]{:S(2)}) collective-permute-start(bf16[128,8192]{0,1:T(8,128)(2,1)} %collective-permute-done.3), channel_id=1, source_target_pairs={{0,128},{8,136},{16,144},{24,152},{32,160},{40,168},{48,176},{56,1... | collective-permute-start | bytes 6291464 | tf_op jit(solution)/shard_map/ppermute | solution.py:12
  368.3 30.5 %copy-start.7 = (bf16[1,256,128]{2,1,0:T(8,128)(2,1)S(1)}, bf16[1,256,128]{2,1,0:T(8,128)(2,1)}, u32[]{:S(2)}) copy-start(bf16[1,256,128]{2,1,0:T(8,128)(2,1)} %param.12) | copy-start | bytes 196612
  391.1 11.9 %collective-permute-start.6 = (bf16[256,1024]{1,0:T(8,128)(2,1)S(1)}, bf16[256,1024]{1,0:T(8,128)(2,1)S(1)}, u32[]{:S(2)}, u32[]{:S(2)}) collective-permute-start(bf16[256,1024]{1,0:T(8,128)(2,1)S(1)} %get-tuple-element.11), channel_id=1, source_target_pairs={{0,8},{8,16},{16,24},{24,32},{32,40},{40,48},{48,56},{56,64},{64,7... | collective-permute-start | bytes 1572872 | tf_op jit(solution)/shard_map/ppermute | solution.py:18
  396.9 10.9 %collective-permute-start.5 = (bf16[256,1024]{1,0:T(8,128)(2,1)S(1)}, bf16[256,1024]{1,0:T(8,128)(2,1)S(1)}, u32[]{:S(2)}, u32[]{:S(2)}) collective-permute-start(bf16[256,1024]{1,0:T(8,128)(2,1)S(1)} %get-tuple-element.12), channel_id=1, source_target_pairs={{8,0},{16,8},{24,16},{32,24},{40,32},{48,40},{56,48},{64,56},{72,6... | collective-permute-start | bytes 1572872 | tf_op jit(solution)/shard_map/ppermute | solution.py:18
  457.0 9.3 %copy-start.1 = (bf16[1,128,8192]{2,1,0:T(8,128)(2,1)S(1)}, bf16[1,128,8192]{2,1,0:T(8,128)(2,1)}, u32[]{:S(2)}) copy-start(bf16[1,128,8192]{2,1,0:T(8,128)(2,1)} %param.8) | copy-start | bytes 6291460
Sparse Core Ops, SparseCore 0:
  11.2 115.5 all-gather.1
  130.9 149.7 reduce-scatter.1
where the time goes:
time: 477 us; the launch traced here: 473 us
  waiting for transfers between devices  369 us (77%)
  other arithmetic  30 us (6%)
  blocking collectives  20.3 us (4%)
  starting transfers between devices  19.1 us (4%)
  between operations  14.1 us (3%)
  matrix products  12.2 us (3%)
  local copies, waits for them, and re-layouts  8.83 us (2%)
    ppermute x5, waiting for transfers between devices, from_partner(): return lax.ppermute(value, axis, pairs)  261 us
    all_gather x1, waiting for transfers between devices, per_device(): full_x = lax.all_gather(rows_x, 'tp', axis=1, tiled=True)  102 us
    psum x1, blocking collectives, per_device(): row_dots = lax.psum(local_dots, 'tp') / full_x.shape[1]  20.3 us
    ppermute x5, starting transfers between devices, from_partner(): return lax.ppermute(value, axis, pairs)  11.3 us
  transfers between devices with their start and end apart: 9, of which 8 were waited for; matrix products, arithmetic and copies ran while one was open for 8% of the time, Pallas kernels for 0%

commit v1 on v0

v1 whole, which is shorter than its diff:
```python
import functools

import jax
import jax.numpy as jnp
from jax import lax
from jax.experimental import pallas as pl
from jax.experimental.pallas import tpu as pltpu
from jax.sharding import PartitionSpec as P

epsilon = 1e-05
MESH = pl.DeviceIdType.MESH
F32 = jnp.float32
BF16 = jnp.bfloat16
N_SEMS = 56


def kernel(
    n_sections,
    w_ref,
    mw_ref,
    xd_ref,
    cd_ref,
    gd_ref,
    xu_ref,
    cu_ref,
    gu_ref,
    wg_ref,
    down_ref,
    up_ref,
    w_all,
    g_all,
    g_scaled,
    x_all,
    x_far,
    c_own,
    part_send,
    part_recv,
    hidden,
    key_send,
    result,
    lanes,
    squares,
    dots,
    ssem,
    rsem,
    lsem,
):
    tok, width = x_far.shape
    keys = gd_ref.shape[2]
    features = width * 8
    tile = min(256, width)
    s = lax.axis_index("section")
    t = lax.axis_index("tp")
    y = t // 2
    h = t % 2
    pair = (s, t + 1 - 2 * h)
    y_peers = [(s, lax.rem(y + k, 4) * 2 + h) for k in range(1, 4)]
    t_peers = [(s, lax.rem(t + k, 8)) for k in range(1, 8)]
    mirror = n_sections - 1 - s
    mirrors = [(mirror, t), (mirror, t + 1 - 2 * h)]
    behind = (lax.rem(s + n_sections - 1, n_sections), t)
    ahead = (lax.rem(s + 1, n_sections), t)

    everyone = t_peers + mirrors + [behind, ahead]
    barrier = pltpu.get_barrier_semaphore()
    for device in everyone:
        pl.semaphore_signal(barrier, inc=1, device_id=device, device_id_type=MESH)

    used = [0]
    used_local = [0]

    def remote(src, dst, device):
        i = used[0]
        used[0] += 1
        return pltpu.make_async_remote_copy(
            src_ref=src,
            dst_ref=dst,
            send_sem=ssem.at[i],
            recv_sem=rsem.at[i],
            device_id=device,
            device_id_type=MESH,
        )

    def local(src, dst):
        i = used_local[0]
        used_local[0] += 1
        copy = pltpu.make_async_copy(src, dst, lsem.at[i])
        copy.start()
        return copy

    def start(copies):
        for copy in copies:
            copy.start()
        return copies

    def wait_recv(copies):
        for copy in copies:
            copy.wait_recv()

    def wait(copies):
        for copy in copies:
            copy.wait()

    own_x = x_all.at[h, pl.ds(0, tok)]
    own_rows = [own_x, x_far]
    copies_x = [local(xd_ref.at[0], own_x), local(xu_ref.at[0], x_far)]
    my_keys = pl.ds(pl.multiple_of(y * keys, keys), keys)
    copies_g = [
        local(gd_ref.at[0], g_all.at[0, :, my_keys]),
        local(gu_ref.at[0], g_all.at[1, :, my_keys]),
    ]
    w_refs = [w_ref, mw_ref]
    halves = [1 - h, h]

    def w_columns(row, half):
        return pl.ds(pl.multiple_of((row * 2 + half) * width, width), width)

    copies_w = [
        [local(w_refs[m].at[0, :, w_columns(y, half)], w_all.at[m, i, my_keys]) for m in range(2)]
        for i, half in enumerate(halves)
    ]
    copies_c = [local(cd_ref.at[0], c_own.at[0]), local(cu_ref.at[0], c_own.at[1])]

    pl.semaphore_wait(barrier, len(everyone))

    g_sends = start(
        [
            remote(ref.at[0], g_all.at[m, :, my_keys], device)
            for m, ref in enumerate((gd_ref, gu_ref))
            for device in y_peers
        ]
    )

    def w_sends(i, m):
        return start(
            [
                remote(
                    w_refs[m].at[0, :, w_columns(lax.rem(y + k + 1, 4), halves[i])],
                    w_all.at[m, i, my_keys],
                    y_peers[k],
                )
                for k in range(3)
            ]
        )

    w_chunks = [w_sends(0, 0), w_sends(0, 1)]
    x_sends = start(
        [
            remote(xd_ref.at[0], x_all.at[h, pl.ds(0, tok)], pair),
            remote(xu_ref.at[0], x_all.at[h, pl.ds(tok, tok)], mirrors[0]),
            remote(xu_ref.at[0], x_all.at[h, pl.ds(tok, tok)], mirrors[1]),
        ]
    )

    def to_row(m):
        return jnp.sum(jnp.transpose(lanes[m]), axis=0, keepdims=True)

    def fold(values):
        total = values[:, :128]
        for i in range(1, values.shape[1] // 128):
            total = total + values[:, i * 128 : (i + 1) * 128]
        return total

    def share(buffer, rows):
        buffer[t] = jnp.broadcast_to(rows, buffer.shape[1:])
        return start([remote(buffer.at[t], buffer.at[t], device) for device in t_peers])

    def total_of(buffer):
        total = buffer[0]
        for i in range(1, 8):
            total = total + buffer[i]
        return total[:1]

    row_block = min(64, tok)
    for m in range(2):
        copies_x[m].wait()

        @pl.loop(0, tok // row_block)
        def _(i):
            rows = pl.ds(pl.multiple_of(i * row_block, row_block), row_block)
            if m == 0:
                values = x_all[h, rows].astype(F32)
            else:
                values = x_far[rows].astype(F32)
            lanes[m, rows] = fold(values * values)

    square_sends = share(squares, jnp.concatenate([to_row(0), to_row(1)], axis=1))

    wait(copies_g)
    wait_recv(g_sends)

    def partial(m, i, use):
        copies_w[i][m].wait()
        wait_recv(w_chunks[i * 2 + m])

        @pl.loop(0, width // tile)
        def _(j):
            columns = pl.ds(pl.multiple_of(j * tile, tile), tile)
            use(columns, jnp.dot(g_all[m], w_all[m, i, :, columns], preferred_element_type=F32))

    part_sends = []
    for m in range(2):

        def keep(columns, value):
            part_send[m, :, columns] = value.astype(BF16)

        partial(m, 0, keep)
        part_sends += start([remote(part_send.at[m], part_recv.at[m], pair)])
        w_chunks.append(w_sends(1, m))

    wait_recv(square_sends)
    inv_rms = lax.rsqrt(total_of(squares) / features + epsilon)
    for m in range(2):
        scale = inv_rms[:, m * tok : (m + 1) * tok]
        for k in range(4):
            block = jnp.transpose(g_all[m, :, k * keys : (k + 1) * keys].astype(F32))
            g_scaled[m, k * keys : (k + 1) * keys] = (block * scale).astype(BF16)
    g_far = start([remote(g_scaled.at[1], g_scaled.at[2], mirrors[0])])

    key_sends = []
    key_own = []

    def key_half(half):
        @pl.loop(0, width // tile)
        def _(j):
            columns = pl.ds(pl.multiple_of(j * tile, tile), tile)
            value = jnp.dot(g_scaled[0], x_all[half, :tok, columns], preferred_element_type=F32)
            value += jnp.dot(g_scaled[2], x_all[half, tok:, columns], preferred_element_type=F32)
            key_send[half, :, columns] = value.astype(BF16)

        place = wg_ref.at[0, :, w_columns(y, half)]
        for k in range(3):
            rows = pl.ds(pl.multiple_of(lax.rem(y + k + 1, 4) * keys, keys), keys)
            key_sends.extend(start([remote(key_send.at[half, rows], place, y_peers[k])]))
        key_own.append(local(key_send.at[half, my_keys], place))

    copies_x_in = x_sends
    wait_recv(copies_x_in)
    wait_recv(g_far)
    key_half(0)

    for m in range(2):

        def finish(columns, value):
            if m == 0:
                x_rows = x_all[h, :tok, columns]
            else:
                x_rows = x_far[:, columns]
            value = value + part_recv[m, :, columns].astype(F32)
            hidden[m, :, columns] = value
            lanes[m] += fold(value * x_rows.astype(F32))

        lanes[m] = jnp.zeros_like(lanes[m])
        part_sends[m].wait_recv()
        partial(m, 1, finish)
    dot_sends = share(dots, jnp.concatenate([to_row(0), to_row(1)], axis=1))
    key_half(1)

    wait(copies_c)
    wait_recv(dot_sends)
    slope = total_of(dots) * (inv_rms * inv_rms * inv_rms) / features

    def to_column(row):
        return jnp.transpose(jnp.broadcast_to(row, (128, row.shape[1])))

    shift_sends = []
    outs = [down_ref, up_ref]
    kept = [s > 0, s < n_sections - 1]
    for m in range(2):
        lanes[0] = to_column(inv_rms[:, m * tok : (m + 1) * tok])
        lanes[1] = to_column(slope[:, m * tok : (m + 1) * tok])

        @pl.loop(0, tok // row_block)
        def _(i):
            rows = pl.ds(pl.multiple_of(i * row_block, row_block), row_block)
            if m == 0:
                x_rows = x_all[h, rows].astype(F32)
            else:
                x_rows = x_far[rows].astype(F32)
            value = c_own[m, rows].astype(F32) + (
                hidden[m, rows] * lanes[0, rows, :1] - x_rows * lanes[1, rows, :1]
            )
            result[m, rows] = jnp.where(kept[m], value, 0.0).astype(BF16)

        shift_sends += start([remote(result.at[m], outs[m].at[0], (behind, ahead)[m])])

    wait_recv(shift_sends)
    wait_recv(key_sends)
    wait(key_own)
    groups = [g_sends, x_sends, square_sends, part_sends, g_far, key_sends, dot_sends, shift_sends] + w_chunks
    for group in groups:
        for copy in group:
            copy.wait_send()


def per_device(*args, n_sections):
    w, _, xd, _, gd = args[:5]
    tok, width = xd.shape[1:]
    keys = gd.shape[2]
    any_spec = pl.BlockSpec(memory_space=pl.ANY)
    vmem = pltpu.VMEM
    outs = pl.pallas_call(
        functools.partial(kernel, n_sections),
        out_shape=(
            jax.ShapeDtypeStruct(w.shape, BF16),
            jax.ShapeDtypeStruct(xd.shape, BF16),
            jax.ShapeDtypeStruct(xd.shape, BF16),
        ),
        in_specs=[any_spec] * 8,
        out_specs=(any_spec,) * 3,
        scratch_shapes=[
            vmem((2, 2, 4 * keys, width), BF16),
            vmem((2, tok, 4 * keys), BF16),
            vmem((3, 4 * keys, tok), BF16),
            vmem((2, 2 * tok, width), BF16),
            vmem((tok, width), BF16),
            vmem((2, tok, width), BF16),
            vmem((2, tok, width), BF16),
            vmem((2, tok, width), BF16),
            vmem((2, tok, width), F32),
            vmem((2, 4 * keys, width), BF16),
            vmem((2, tok, width), BF16),
            vmem((2, tok, 128), F32),
            vmem((8, 8, 2 * tok), F32),
            vmem((8, 8, 2 * tok), F32),
            pltpu.SemaphoreType.DMA((N_SEMS,)),
            pltpu.SemaphoreType.DMA((N_SEMS,)),
            pltpu.SemaphoreType.DMA((16,)),
        ],
        compiler_params=pltpu.CompilerParams(
            collective_id=0, has_side_effects=True, vmem_limit_bytes=40 * 2**20
        ),
        name="relay_backward",
    )(*args)
    return outs


def solution(mesh):
    keys_split = P("section", "tp", None)
    features_split = P("section", None, "tp")
    return jax.shard_map(
        functools.partial(per_device, n_sections=mesh.shape["section"]),
        mesh=mesh,
        in_specs=(keys_split,) * 2 + (features_split,) * 6,
        out_specs=(keys_split, features_split, features_split),
        check_vma=False,
    )
```

time: 477 us -> 118 us (0.25)
  waiting for transfers between devices: 369 us -> 0 us
  Pallas kernels: 0 us -> 105 us
  other arithmetic: 30 us -> 0 us
  blocking collectives: 20.3 us -> 0 us
  starting transfers between devices: 19.1 us -> 0 us
  between operations: 14.1 us -> 0.66 us
  matrix products: 12.2 us -> 0 us
    ppermute x7 -> x0, waiting for transfers between devices: 267 us -> none  [the longest x5 261 us: from_partner(): return lax.ppermute(value, axis, pairs)]
    pallas_call x0 -> x1, Pallas kernels: none -> 105 us  [per_device(): pl.pallas_call(functools.partial(kernel, n_sections), out_shape=(jax.Shap...]
    all_gather x1 -> x0, waiting for transfers between devices: 102 us -> none  [per_device(): full_x = lax.all_gather(rows_x, 'tp', axis=1, tiled=True)]
    psum x1 -> x0, blocking collectives: 20.3 us -> none  [per_device(): row_dots = lax.psum(local_dots, 'tp') / full_x.shape[1]]
    ppermute x7 -> x0, starting transfers between devices: 19 us -> none  [the longest x5 11.3 us: from_partner(): return lax.ppermute(value, axis, pairs)]
    dot_general x4 -> x0, matrix products: 12.2 us -> none  [the longest x2 4.82 us: key_product(): lax.dot_general(cot_rows, normed_rows, (((0,), (0,)), ((), ())), preferre...]
    concatenate x2 -> x0, other arithmetic: 10.1 us -> none  [the longest x1 7.67 us: per_device(): partial_value_term = jnp.concatenate([part_near, distant_portion], axis=0)]
    reduce_sum x2 -> x0, other arithmetic: 7.45 us -> none  [the longest x1 5.25 us: per_device(): jnp.mean(inputs * inputs, axis=1, keepdims=True) + epsilon]
  transfers between devices with their start and end apart: 9 -> 0, of which waited for: 8 -> 0; matrix products, arithmetic and copies ran while one was open for 8% -> 0% of each run, Pallas kernels for 0% -> 0%
where the time goes in v1:
time: 118 us
  Pallas kernels  105 us (89%)
  local copies, waits for them, and re-layouts  11.9 us (10%)
    pallas_call x1, Pallas kernels, per_device(): pl.pallas_call(functools.partial(kernel, n_sections), out_shape=(jax.Shap...  105 us
    unnamed x19, local copies, waits for them, and re-layouts  11.9 us

profile of v1, /device:TPU:1, one launch (start us, length us, event | category | flops | bytes accessed | tf_op | source)
XLA Modules:
  0.0 117.8 jit_solution(8857463111125526225)
XLA Ops:
  0.6 0.0 copy-start
  0.6 1.6 %copy-done = bf16[1,128,8192]{2,1,0:T(8,128)(2,1)S(1)} copy-done((bf16[1,128,8192]{2,1,0:T(8,128)(2,1)S(1)}, bf16[1,128,8192]{2,1,0:T(8,128)(2,1)}, u32[]{:S(2)}) %copy-start) | copy-done | bytes 2097176
  2.2 0.0 copy-start.1
  2.2 1.6 %copy-done.1 = bf16[1,128,8192]{2,1,0:T(8,128)(2,1)S(1)} copy-done((bf16[1,128,8192]{2,1,0:T(8,128)(2,1)S(1)}, bf16[1,128,8192]{2,1,0:T(8,128)(2,1)}, u32[]{:S(2)}) %copy-start.1) | copy-done | bytes 2097176
  3.8 0.0 copy-start.2
  3.8 1.0 copy-done.2
  4.9 0.0 copy-start.3
  4.9 1.0 copy-done.3
  5.9 0.0 copy-start.4
  5.9 1.0 copy-done.4
  6.9 0.0 copy-start.5
  6.9 1.0 copy-done.5
  8.0 0.0 copy-start.6
  8.0 0.8 copy-done.6
  8.8 0.0 copy-start.7
  8.8 0.8 copy-done.7
  9.7 105.2 %relay_backward.1 = (bf16[1,128,8192]{2,1,0:T(8,128)(2,1)S(1)}, bf16[1,256,1024]{2,1,0:T(8,128)(2,1)S(1)}, bf16[1,256,1024]{2,1,0:T(8,128)(2,1)S(1)}) custom-call(bf16[1,128,8192]{2,1,0:T(8,128)(2,1)S(1)} %copy-done, bf16[1,128,8192]{2,1,0:T(8,128)(2,1)S(1)} %copy-done.1, bf16[1,256,1024]{2,1,0:T(8,128)(2,1)S(1)} %copy-done.2, ...), custom_call_target="tpu_custom_call" | custom-call | tf_op jit(solution)/shard_map/relay_backward/pallas_call | solution.py:302
  114.9 1.3 %copy.14 = bf16[1,128,8192]{2,1,0:T(8,128)(2,1)} copy(bf16[1,128,8192]{2,1,0:T(8,128)(2,1)S(1)} %get-tuple-element.6) | data formatting | bytes 4194304
  116.2 0.8 copy.15
  117.0 0.8 copy.16
Async XLA Ops:
  0.6 1.6 %copy-start = (bf16[1,128,8192]{2,1,0:T(8,128)(2,1)S(1)}, bf16[1,128,8192]{2,1,0:T(8,128)(2,1)}, u32[]{:S(2)}) copy-start(bf16[1,128,8192]{2,1,0:T(8,128)(2,1)} %w_ref.1) | copy-start | bytes 6291460
  2.2 1.6 %copy-start.1 = (bf16[1,128,8192]{2,1,0:T(8,128)(2,1)S(1)}, bf16[1,128,8192]{2,1,0:T(8,128)(2,1)}, u32[]{:S(2)}) copy-start(bf16[1,128,8192]{2,1,0:T(8,128)(2,1)} %mw_ref.1) | copy-start | bytes 6291460
  3.8 1.0 copy-start.2
  4.9 1.0 copy-start.3
  5.9 1.0 copy-start.4
  6.9 1.0 copy-start.5
  8.0 0.8 copy-start.6
  8.8 0.8 copy-start.7

commit v2 on v1

--- a/solution.py
+++ b/solution.py
@@ -9,9 +9,11 @@
 
 epsilon = 1e-05
 MESH = pl.DeviceIdType.MESH
+PIECES = 4
+DEPTH = 2
 F32 = jnp.float32
 BF16 = jnp.bfloat16
-N_SEMS = 56
+N_SEMS = 96
 
 
 def kernel(
@@ -49,6 +51,7 @@
     keys = gd_ref.shape[2]
     features = width * 8
     tile = min(256, width)
+    groups = 2 * tok // 128
     s = lax.axis_index("section")
     t = lax.axis_index("tp")
     y = t // 2
@@ -123,6 +126,14 @@
 
     pl.semaphore_wait(barrier, len(everyone))
 
+    x_sends = start(
+        [
+            remote(xd_ref.at[0], x_all.at[h, pl.ds(0, tok)], pair),
+            remote(xu_ref.at[0], x_all.at[h, pl.ds(tok, tok)], mirrors[0]),
+            remote(xu_ref.at[0], x_all.at[h, pl.ds(tok, tok)], mirrors[1]),
+        ]
+    )
+
     g_sends = start(
         [
             remote(ref.at[0], g_all.at[m, :, my_keys], device)
@@ -144,14 +155,6 @@
         )
 
     w_chunks = [w_sends(0, 0), w_sends(0, 1)]
-    x_sends = start(
-        [
-            remote(xd_ref.at[0], x_all.at[h, pl.ds(0, tok)], pair),
-            remote(xu_ref.at[0], x_all.at[h, pl.ds(tok, tok)], mirrors[0]),
-            remote(xu_ref.at[0], x_all.at[h, pl.ds(tok, tok)], mirrors[1]),
-        ]
-    )
-
     def to_row(m):
         return jnp.sum(jnp.transpose(lanes[m]), axis=0, keepdims=True)
 
@@ -161,15 +164,15 @@
             total = total + values[:, i * 128 : (i + 1) * 128]
         return total
 
-    def share(buffer, rows):
-        buffer[t] = jnp.broadcast_to(rows, buffer.shape[1:])
+    def share(buffer, row):
+        buffer[t, :groups] = jnp.concatenate([row[:, i * 128 : (i + 1) * 128] for i in range(groups)], axis=0)
         return start([remote(buffer.at[t], buffer.at[t], device) for device in t_peers])
 
     def total_of(buffer):
         total = buffer[0]
         for i in range(1, 8):
             total = total + buffer[i]
-        return total[:1]
+        return jnp.concatenate([total[i : i + 1] for i in range(groups)], axis=1)
 
     row_block = min(64, tok)
     for m in range(2):
@@ -191,7 +194,8 @@
 
     def partial(m, i, use):
         copies_w[i][m].wait()
-        wait_recv(w_chunks[i * 2 + m])
+        if (m, i) != (1, 1):
+            wait_recv(w_chunks[i * 2 + m])
 
         @pl.loop(0, width // tile)
         def _(j):
@@ -200,13 +204,11 @@
 
     part_sends = []
     for m in range(2):
-
-        def keep(columns, value):
-            part_send[m, :, columns] = value.astype(BF16)
-
-        partial(m, 0, keep)
-        part_sends += start([remote(part_send.at[m], part_recv.at[m], pair)])
-        w_chunks.append(w_sends(1, m))
+      def keep(columns, value):
+          part_send[m, :, columns] = value.astype(BF16)
+      partial(m, 0, keep)
+      part_sends += start([remote(part_send.at[m], part_recv.at[m], pair)])
+      w_chunks.append(w_sends(1, m))
 
     wait_recv(square_sends)
     inv_rms = lax.rsqrt(total_of(squares) / features + epsilon)
@@ -217,30 +219,7 @@
             g_scaled[m, k * keys : (k + 1) * keys] = (block * scale).astype(BF16)
     g_far = start([remote(g_scaled.at[1], g_scaled.at[2], mirrors[0])])
 
-    key_sends = []
-    key_own = []
-
-    def key_half(half):
-        @pl.loop(0, width // tile)
-        def _(j):
-            columns = pl.ds(pl.multiple_of(j * tile, tile), tile)
-            value = jnp.dot(g_scaled[0], x_all[half, :tok, columns], preferred_element_type=F32)
-            value += jnp.dot(g_scaled[2], x_all[half, tok:, columns], preferred_element_type=F32)
-            key_send[half, :, columns] = value.astype(BF16)
-
-        place = wg_ref.at[0, :, w_columns(y, half)]
-        for k in range(3):
-            rows = pl.ds(pl.multiple_of(lax.rem(y + k + 1, 4) * keys, keys), keys)
-            key_sends.extend(start([remote(key_send.at[half, rows], place, y_peers[k])]))
-        key_own.append(local(key_send.at[half, my_keys], place))
-
-    copies_x_in = x_sends
-    wait_recv(copies_x_in)
-    wait_recv(g_far)
-    key_half(0)
-
-    for m in range(2):
-
+    def own_half(m):
         def finish(columns, value):
             if m == 0:
                 x_rows = x_all[h, :tok, columns]
@@ -253,9 +232,56 @@
         lanes[m] = jnp.zeros_like(lanes[m])
         part_sends[m].wait_recv()
         partial(m, 1, finish)
+
+    def key_half(half):
+        @pl.loop(0, width // tile)
+        def _(j):
+            columns = pl.ds(pl.multiple_of(j * tile, tile), tile)
+            value = jnp.dot(g_scaled[0], x_all[half, :tok, columns], preferred_element_type=F32)
+            value += jnp.dot(g_scaled[2], x_all[half, tok:, columns], preferred_element_type=F32)
+            key_send[half, :, columns] = value.astype(BF16)
+
+    key_sends = []
+    key_own = []
+    key_queue = []
+
+    def key_out(half):
+        place = wg_ref.at[0, :, w_columns(y, half)]
+        for piece in range(PIECES):
+            size = width // PIECES
+            columns = pl.ds(piece * size, size)
+            group = []
+            for k in range(3):
+                rows = pl.ds(pl.multiple_of(lax.rem(y + k + 1, 4) * keys, keys), keys)
+                group.append(remote(key_send.at[half, rows, columns], place.at[:, columns], y_peers[k]))
+            key_queue.append(group)
+        key_own.append(local(key_send.at[half, my_keys], place))
+
+    def pump(count=1, fresh=False):
+        for _ in range(count):
+            if not key_queue:
+                return
+            if not fresh:
+                for copy in key_sends[-3 * DEPTH : len(key_sends) - 3 * (DEPTH - 1)]:
+                    copy.wait_send()
+                    sent.append(copy)
+            key_sends.extend(start(key_queue.pop(0)))
+
+    sent = []
+
+    wait_recv(x_sends)
+    wait_recv(g_far)
+    key_half(0)
+    key_out(0)
+    key_half(1)
+    key_out(1)
+    own_half(0)
+    pump(1, True)
+    wait_recv(w_chunks[3])
+    pump(DEPTH - 1, True)
+    own_half(1)
     dot_sends = share(dots, jnp.concatenate([to_row(0), to_row(1)], axis=1))
-    key_half(1)
-
+    pump(3)
     wait(copies_c)
     wait_recv(dot_sends)
     slope = total_of(dots) * (inv_rms * inv_rms * inv_rms) / features
@@ -283,6 +309,8 @@
             result[m, rows] = jnp.where(kept[m], value, 0.0).astype(BF16)
 
         shift_sends += start([remote(result.at[m], outs[m].at[0], (behind, ahead)[m])])
+        pump(1)
+    pump(len(key_queue))
 
     wait_recv(shift_sends)
     wait_recv(key_sends)
@@ -290,15 +318,18 @@
     groups = [g_sends, x_sends, square_sends, part_sends, g_far, key_sends, dot_sends, shift_sends] + w_chunks
     for group in groups:
         for copy in group:
-            copy.wait_send()
+            if not any(copy is other for other in sent):
+                copy.wait_send()
 
 
 def per_device(*args, n_sections):
     w, _, xd, _, gd = args[:5]
     tok, width = xd.shape[1:]
     keys = gd.shape[2]
+    hbm_spec = pl.BlockSpec(memory_space=pltpu.HBM)
     any_spec = pl.BlockSpec(memory_space=pl.ANY)
     vmem = pltpu.VMEM
+    args = [pltpu.with_memory_space_constraint(a, pltpu.HBM) for a in args]
     outs = pl.pallas_call(
         functools.partial(kernel, n_sections),
         out_shape=(
@@ -306,7 +337,7 @@
             jax.ShapeDtypeStruct(xd.shape, BF16),
             jax.ShapeDtypeStruct(xd.shape, BF16),
         ),
-        in_specs=[any_spec] * 8,
+        in_specs=[hbm_spec] * 8,
         out_specs=(any_spec,) * 3,
         scratch_shapes=[
             vmem((2, 2, 4 * keys, width), BF16),
@@ -321,11 +352,11 @@
             vmem((2, 4 * keys, width), BF16),
             vmem((2, tok, width), BF16),
             vmem((2, tok, 128), F32),
-            vmem((8, 8, 2 * tok), F32),
-            vmem((8, 8, 2 * tok), F32),
+            vmem((8, 8, 128), F32),
+            vmem((8, 8, 128), F32),
             pltpu.SemaphoreType.DMA((N_SEMS,)),
             pltpu.SemaphoreType.DMA((N_SEMS,)),
-            pltpu.SemaphoreType.DMA((16,)),
+            pltpu.SemaphoreType.DMA((32,)),
         ],
         compiler_params=pltpu.CompilerParams(
             collective_id=0, has_side_effects=True, vmem_limit_bytes=40 * 2**20

time: 118 us -> 108 us (0.915)
  local copies, waits for them, and re-layouts: 11.9 us -> 2.91 us
    unnamed x19 -> x3, local copies, waits for them, and re-layouts: 11.9 us -> 2.91 us
where the time goes in v2:
time: 108 us
  Pallas kernels  104 us (96%)
  local copies, waits for them, and re-layouts  2.91 us (3%)
    pallas_call x1, Pallas kernels, per_device(): pl.pallas_call(functools.partial(kernel, n_sections), out_shape=(jax.Shap...  104 us
    unnamed x3, local copies, waits for them, and re-layouts  2.91 us

profile of v2, /device:TPU:1, one launch (start us, length us, event | category | flops | bytes accessed | tf_op | source)
XLA Modules:
  0.0 107.8 jit_solution(12909057065834618869)
XLA Ops:
  0.6 104.3 %relay_backward.1 = (bf16[1,128,8192]{2,1,0:T(8,128)(2,1)S(1)}, bf16[1,256,1024]{2,1,0:T(8,128)(2,1)S(1)}, bf16[1,256,1024]{2,1,0:T(8,128)(2,1)S(1)}) custom-call(bf16[1,128,8192]{2,1,0:T(8,128)(2,1)} %w_ref.1, bf16[1,128,8192]{2,1,0:T(8,128)(2,1)} %mw_ref.1, bf16[1,256,1024]{2,1,0:T(8,128)(2,1)} %xd_ref.1, bf16[1,256,1024]{2,1,0:T(8,128)(2,1)} %cd_ref.1, ...), custom_call_target="tpu_custom_call" | custom-call | tf_op jit(solution)/shard_map/relay_backward/pallas_call | solution.py:333
  104.9 1.3 %copy.14 = bf16[1,128,8192]{2,1,0:T(8,128)(2,1)} copy(bf16[1,128,8192]{2,1,0:T(8,128)(2,1)S(1)} %get-tuple-element.6) | data formatting | bytes 4194304
  106.2 0.8 copy.15
  107.0 0.8 copy.16

commit v3 on v2

--- a/solution.py
+++ b/solution.py
@@ -9,11 +9,12 @@
 
 epsilon = 1e-05
 MESH = pl.DeviceIdType.MESH
-PIECES = 4
-DEPTH = 2
+K_PIECES = 8
+X_PIECES = 4
+DEPTH = 4
 F32 = jnp.float32
 BF16 = jnp.bfloat16
-N_SEMS = 96
+N_SEMS = 128
 
 
 def kernel(
@@ -34,6 +35,7 @@
     g_scaled,
     x_all,
     x_far,
+    x_relay,
     c_own,
     part_send,
     part_recv,
@@ -46,12 +48,13 @@
     ssem,
     rsem,
     lsem,
+    ack,
 ):
     tok, width = x_far.shape
     keys = gd_ref.shape[2]
     features = width * 8
     tile = min(256, width)
-    groups = 2 * tok // 128
+    groups = tok // 128
     s = lax.axis_index("section")
     t = lax.axis_index("tp")
     y = t // 2
@@ -60,14 +63,31 @@
     y_peers = [(s, lax.rem(y + k, 4) * 2 + h) for k in range(1, 4)]
     t_peers = [(s, lax.rem(t + k, 8)) for k in range(1, 8)]
     mirror = n_sections - 1 - s
-    mirrors = [(mirror, t), (mirror, t + 1 - 2 * h)]
+    mirrored = (mirror, t)
+    z = s // 4
+    turned = 8 * z + 3 - s
+    relays = [(turned, t), (turned, t + 1 - 2 * h)]
+    across_s = n_sections - 4 - 8 * z + s
+    across = (across_s, t)
     behind = (lax.rem(s + n_sections - 1, n_sections), t)
     ahead = (lax.rem(s + 1, n_sections), t)
 
-    everyone = t_peers + mirrors + [behind, ahead]
+    others = [(s, k * 2 + 1 - h) for k in range(4)]
+
     barrier = pltpu.get_barrier_semaphore()
-    for device in everyone:
-        pl.semaphore_signal(barrier, inc=1, device_id=device, device_id_type=MESH)
+    low_half = h == 0
+    low_mirror = s < n_sections // 2
+    low_relay = s < turned
+
+    def signal(semaphore, devices):
+        for device in devices:
+            pl.semaphore_signal(semaphore, inc=1, device_id=device, device_id_type=MESH)
+
+    signal(barrier, y_peers)
+    pl.when(low_half)(lambda: signal(barrier, others))
+    pl.when(low_relay)(lambda: signal(barrier, relays))
+    pl.when(low_mirror)(lambda: signal(barrier, [mirrored, across]))
+    pl.when(s < n_sections - 1)(lambda: signal(barrier, [ahead]))
 
     used = [0]
     used_local = [0]
@@ -104,6 +124,24 @@
         for copy in copies:
             copy.wait()
 
+    y_queue = []
+    y_started = []
+    sent = []
+
+    def pump(count=1):
+        for _ in range(count):
+            if len(y_started) >= DEPTH:
+                for copy in y_started[-DEPTH]:
+                    copy.wait_send()
+                    sent.append(copy)
+            y_started.append(start(y_queue.pop(0)))
+
+    def cut(pieces, size):
+        return [pl.ds(i * (size // pieces), size // pieces) for i in range(pieces)]
+
+    def remote_cut(pieces, src, dst, device):
+        return [remote(src.at[rows], dst.at[rows], device) for rows in cut(pieces, src.shape[0])]
+
     own_x = x_all.at[h, pl.ds(0, tok)]
     own_rows = [own_x, x_far]
     copies_x = [local(xd_ref.at[0], own_x), local(xu_ref.at[0], x_far)]
@@ -124,15 +162,7 @@
     ]
     copies_c = [local(cd_ref.at[0], c_own.at[0]), local(cu_ref.at[0], c_own.at[1])]
 
-    pl.semaphore_wait(barrier, len(everyone))
-
-    x_sends = start(
-        [
-            remote(xd_ref.at[0], x_all.at[h, pl.ds(0, tok)], pair),
-            remote(xu_ref.at[0], x_all.at[h, pl.ds(tok, tok)], mirrors[0]),
-            remote(xu_ref.at[0], x_all.at[h, pl.ds(tok, tok)], mirrors[1]),
-        ]
-    )
+    pl.semaphore_wait(barrier, 3 + jnp.where(low_half, 0, 4) + jnp.where(low_relay, 0, 2) + jnp.where(low_mirror, 0, 2) + jnp.where(s > 0, 1, 0))
 
     g_sends = start(
         [
@@ -141,8 +171,12 @@
             for device in y_peers
         ]
     )
-
-    def w_sends(i, m):
+    pl.when(h == 1)(lambda: signal(ack.at[0], others))
+    pl.when(s > turned)(lambda: signal(ack.at[3], relays))
+    pl.when(s >= n_sections // 2)(lambda: signal(ack.at[1], [mirrored, across]))
+    pl.when(s > 0)(lambda: signal(ack.at[2], [behind]))
+
+    def w_sends(m, i):
         return start(
             [
                 remote(
@@ -154,7 +188,6 @@
             ]
         )
 
-    w_chunks = [w_sends(0, 0), w_sends(0, 1)]
     def to_row(m):
         return jnp.sum(jnp.transpose(lanes[m]), axis=0, keepdims=True)
 
@@ -165,14 +198,24 @@
         return total
 
     def share(buffer, row):
+        groups = row.shape[1] // 128
         buffer[t, :groups] = jnp.concatenate([row[:, i * 128 : (i + 1) * 128] for i in range(groups)], axis=0)
         return start([remote(buffer.at[t], buffer.at[t], device) for device in t_peers])
 
-    def total_of(buffer):
+    def total_of(buffer, groups):
         total = buffer[0]
         for i in range(1, 8):
             total = total + buffer[i]
         return jnp.concatenate([total[i : i + 1] for i in range(groups)], axis=1)
+
+    pl.when(low_half)(lambda: pl.semaphore_wait(ack.at[0], 4))
+    pl.when(low_relay)(lambda: pl.semaphore_wait(ack.at[3], 2))
+    row_halves = cut(2, tok)
+    x_turned = []
+    for i in range(2):
+        x_turned.append(remote_cut(2, xu_ref.at[0, row_halves[i]], x_relay.at[row_halves[i]], relays[i]))
+    for i in range(2):
+        start([x_turned[1][i], x_turned[0][i]])
 
     row_block = min(64, tok)
     for m in range(2):
@@ -188,37 +231,54 @@
             lanes[m, rows] = fold(values * values)
 
     square_sends = share(squares, jnp.concatenate([to_row(0), to_row(1)], axis=1))
+    w_chunks = {(m, i): w_sends(m, i) for i in range(2) for m in range(2)}
+    far_rows = [x_all.at[(h, 1 - h)[i], pl.ds(tok + rows.start, rows.size)] for i, rows in enumerate(row_halves)]
+    x_mirror = [remote_cut(2, x_relay.at[row_halves[i]], far_rows[i], across) for i in range(2)]
+    pl.when(low_mirror)(lambda: pl.semaphore_wait(ack.at[1], 2))
+    for i in range(2):
+        x_turned[1][i].wait_recv()
+        x_mirror[1][i].start()
+
+    wait_recv(x_turned[0])
+    x_near = start(remote_cut(X_PIECES, xd_ref.at[0], own_x, pair))
 
     wait(copies_g)
     wait_recv(g_sends)
 
     def partial(m, i, use):
         copies_w[i][m].wait()
-        if (m, i) != (1, 1):
-            wait_recv(w_chunks[i * 2 + m])
+        wait_recv(w_chunks[m, i])
 
         @pl.loop(0, width // tile)
         def _(j):
             columns = pl.ds(pl.multiple_of(j * tile, tile), tile)
             use(columns, jnp.dot(g_all[m], w_all[m, i, :, columns], preferred_element_type=F32))
 
+    def scale_g():
+        wait_recv(square_sends)
+        inv_rms = lax.rsqrt(total_of(squares, 2 * groups) / features + epsilon)
+        for m in range(2):
+            scale = inv_rms[:, m * tok : (m + 1) * tok]
+            for k in range(4):
+                block = jnp.transpose(g_all[m, :, k * keys : (k + 1) * keys].astype(F32))
+                g_scaled[m, k * keys : (k + 1) * keys] = (block * scale).astype(BF16)
+        return inv_rms
+
+    inv_rms = scale_g()
     part_sends = []
     for m in range(2):
-      def keep(columns, value):
-          part_send[m, :, columns] = value.astype(BF16)
-      partial(m, 0, keep)
-      part_sends += start([remote(part_send.at[m], part_recv.at[m], pair)])
-      w_chunks.append(w_sends(1, m))
-
-    wait_recv(square_sends)
-    inv_rms = lax.rsqrt(total_of(squares) / features + epsilon)
-    for m in range(2):
-        scale = inv_rms[:, m * tok : (m + 1) * tok]
-        for k in range(4):
-            block = jnp.transpose(g_all[m, :, k * keys : (k + 1) * keys].astype(F32))
-            g_scaled[m, k * keys : (k + 1) * keys] = (block * scale).astype(BF16)
-    g_far = start([remote(g_scaled.at[1], g_scaled.at[2], mirrors[0])])
-
+
+        def keep(columns, value):
+            part_send[m, :, columns] = value.astype(BF16)
+
+        if m == 1:
+            wait_recv(x_mirror[1])
+            x_pair = [start(remote_cut(2, far_rows[1], far_rows[1], pair))]
+        partial(m, 0, keep)
+        part_sends.append(start(remote_cut(X_PIECES, part_send.at[m], part_recv.at[m], pair)))
+        if m == 0:
+            start(x_mirror[0])
+            g_far = start([remote(g_scaled.at[1], g_scaled.at[2], mirrored)])
     def own_half(m):
         def finish(columns, value):
             if m == 0:
@@ -230,7 +290,7 @@
             lanes[m] += fold(value * x_rows.astype(F32))
 
         lanes[m] = jnp.zeros_like(lanes[m])
-        part_sends[m].wait_recv()
+        wait_recv(part_sends[m])
         partial(m, 1, finish)
 
     def key_half(half):
@@ -243,48 +303,17 @@
 
     key_sends = []
     key_own = []
-    key_queue = []
 
     def key_out(half):
         place = wg_ref.at[0, :, w_columns(y, half)]
-        for piece in range(PIECES):
-            size = width // PIECES
-            columns = pl.ds(piece * size, size)
+        for rows in cut(K_PIECES, keys):
             group = []
             for k in range(3):
-                rows = pl.ds(pl.multiple_of(lax.rem(y + k + 1, 4) * keys, keys), keys)
-                group.append(remote(key_send.at[half, rows, columns], place.at[:, columns], y_peers[k]))
-            key_queue.append(group)
+                mine = pl.ds(pl.multiple_of(lax.rem(y + k + 1, 4) * keys + rows.start, rows.size), rows.size)
+                group.append(remote(key_send.at[half, mine], place.at[rows], y_peers[k]))
+            y_queue.append(group)
+            key_sends.extend(group)
         key_own.append(local(key_send.at[half, my_keys], place))
-
-    def pump(count=1, fresh=False):
-        for _ in range(count):
-            if not key_queue:
-                return
-            if not fresh:
-                for copy in key_sends[-3 * DEPTH : len(key_sends) - 3 * (DEPTH - 1)]:
-                    copy.wait_send()
-                    sent.append(copy)
-            key_sends.extend(start(key_queue.pop(0)))
-
-    sent = []
-
-    wait_recv(x_sends)
-    wait_recv(g_far)
-    key_half(0)
-    key_out(0)
-    key_half(1)
-    key_out(1)
-    own_half(0)
-    pump(1, True)
-    wait_recv(w_chunks[3])
-    pump(DEPTH - 1, True)
-    own_half(1)
-    dot_sends = share(dots, jnp.concatenate([to_row(0), to_row(1)], axis=1))
-    pump(3)
-    wait(copies_c)
-    wait_recv(dot_sends)
-    slope = total_of(dots) * (inv_rms * inv_rms * inv_rms) / features
 
     def to_column(row):
         return jnp.transpose(jnp.broadcast_to(row, (128, row.shape[1])))
@@ -292,9 +321,13 @@
     shift_sends = []
     outs = [down_ref, up_ref]
     kept = [s > 0, s < n_sections - 1]
-    for m in range(2):
-        lanes[0] = to_column(inv_rms[:, m * tok : (m + 1) * tok])
-        lanes[1] = to_column(slope[:, m * tok : (m + 1) * tok])
+
+    def finish_rows(m):
+        wait_recv(dot_sends[m])
+        copies_c[m].wait()
+        scale = inv_rms[:, m * tok : (m + 1) * tok]
+        lanes[0] = to_column(scale)
+        lanes[1] = to_column(total_of(dots.at[m], groups) * (scale * scale * scale) / features)
 
         @pl.loop(0, tok // row_block)
         def _(i):
@@ -308,18 +341,59 @@
             )
             result[m, rows] = jnp.where(kept[m], value, 0.0).astype(BF16)
 
-        shift_sends += start([remote(result.at[m], outs[m].at[0], (behind, ahead)[m])])
-        pump(1)
-    pump(len(key_queue))
-
+        if m == 1:
+            pl.when(s < n_sections - 1)(lambda: pl.semaphore_wait(ack.at[2], 1))
+        shift_sends.extend(start([remote(result.at[m], outs[m].at[0], (behind, ahead)[m])]))
+
+    own_half(0)
+    dot_sends = [share(dots.at[0], to_row(0))]
+    wait_recv(x_mirror[0])
+    x_pair.append(start(remote_cut(2, far_rows[0], far_rows[0], pair)))
+    wait_recv(g_far)
+    wait_recv(x_pair[0])
+    key_half(h)
+    key_out(h)
+    pump(DEPTH)
+    own_half(1)
+    dot_sends.append(share(dots.at[1], to_row(1)))
+    pump(2)
+    finish_rows(0)
+    pump(2)
+    wait_recv(x_near)
+    wait_recv(x_pair[1])
+    key_half(1 - h)
+    key_out(1 - h)
+    pump(2)
+    finish_rows(1)
+    pump(len(y_queue))
     wait_recv(shift_sends)
     wait_recv(key_sends)
     wait(key_own)
-    groups = [g_sends, x_sends, square_sends, part_sends, g_far, key_sends, dot_sends, shift_sends] + w_chunks
+    groups = [g_sends, x_near, *x_turned, *x_mirror, *x_pair, square_sends, *part_sends, g_far, key_sends, *dot_sends, shift_sends, *w_chunks.values()]
     for group in groups:
         for copy in group:
             if not any(copy is other for other in sent):
                 copy.wait_send()
+
+
+def place(values):
+    def body(*refs):
+        sems = refs[-1]
+        copies = [pltpu.make_async_copy(refs[i], refs[i + 3], sems.at[i]) for i in range(3)]
+        for copy in copies:
+            copy.start()
+        for copy in copies:
+            copy.wait()
+
+    return pl.pallas_call(
+        body,
+        out_shape=tuple(jax.ShapeDtypeStruct(v.shape, v.dtype) for v in values),
+        in_specs=[pl.BlockSpec(memory_space=pl.ANY)] * 3,
+        out_specs=(pl.BlockSpec(memory_space=pltpu.HBM),) * 3,
+        scratch_shapes=[pltpu.SemaphoreType.DMA((3,))],
+        compiler_params=pltpu.CompilerParams(vmem_limit_bytes=2**20),
+        name="place",
+    )(*values)
 
 
 def per_device(*args, n_sections):
@@ -345,6 +419,7 @@
             vmem((3, 4 * keys, tok), BF16),
             vmem((2, 2 * tok, width), BF16),
             vmem((tok, width), BF16),
+            vmem((tok, width), BF16),
             vmem((2, tok, width), BF16),
             vmem((2, tok, width), BF16),
             vmem((2, tok, width), BF16),
@@ -353,17 +428,18 @@
             vmem((2, tok, width), BF16),
             vmem((2, tok, 128), F32),
             vmem((8, 8, 128), F32),
-            vmem((8, 8, 128), F32),
+            vmem((2, 8, 8, 128), F32),
             pltpu.SemaphoreType.DMA((N_SEMS,)),
             pltpu.SemaphoreType.DMA((N_SEMS,)),
-            pltpu.SemaphoreType.DMA((32,)),
+            pltpu.SemaphoreType.DMA((16,)),
+            pltpu.SemaphoreType.REGULAR((4,)),
         ],
         compiler_params=pltpu.CompilerParams(
             collective_id=0, has_side_effects=True, vmem_limit_bytes=40 * 2**20
         ),
         name="relay_backward",
     )(*args)
-    return outs
+    return place(outs)
 
 
 def solution(mesh):

time: 108 us -> 93 us (0.86)
  the two profiles are of different devices: /device:TPU:1 before, /device:TPU:224 now
where the time goes in v3:
time: 93 us; the launch traced here: 92.9 us
  Pallas kernels  92.3 us (99%)
    pallas_call x1, Pallas kernels, per_device(): pl.pallas_call(functools.partial(kernel, n_sections), out_shape=(jax.Shap...  90.6 us

profile of v3, /device:TPU:224, one launch (start us, length us, event | category | flops | bytes accessed | tf_op | source)
XLA Modules:
  0.0 92.9 jit_solution(18287958140166183444)
XLA Ops:
  0.6 90.6 %relay_backward.1 = (bf16[1,128,8192]{2,1,0:T(8,128)(2,1)S(1)}, bf16[1,256,1024]{2,1,0:T(8,128)(2,1)S(1)}, bf16[1,256,1024]{2,1,0:T(8,128)(2,1)S(1)}) custom-call(bf16[1,128,8192]{2,1,0:T(8,128)(2,1)} %w_ref.1, bf16[1,128,8192]{2,1,0:T(8,128)(2,1)} %mw_ref.1, bf16[1,256,1024]{2,1,0:T(8,128)(2,1)} %xd_ref.1, bf16[1,256,1024]{2,1,0:T(8,128)(2,1)} %cd_ref.1, ...), custom_call_target="tpu_custom_call" | custom-call | tf_op jit(solution)/shard_map/relay_backward/pallas_call | solution.py:407
  91.3 1.7 %place.1 = (bf16[1,128,8192]{2,1,0:T(8,128)(2,1)}, bf16[1,256,1024]{2,1,0:T(8,128)(2,1)}, bf16[1,256,1024]{2,1,0:T(8,128)(2,1)}) custom-call(bf16[1,128,8192]{2,1,0:T(8,128)(2,1)S(1)} %get-tuple-element.6.refs_0_, bf16[1,256,1024]{2,1,0:T(8,128)(2,1)S(1)} %get-tuple-element.7.refs_1_, bf16[1,256,1024]{2,1,0:T(8,128)(2,1)S(1)} %get-tuple-element.8.refs_2_), custom_call_target="tpu_custom_call" | custom-call | tf_op jit(solution)/shard_map/place/pallas_call | solution.py:388

commit v4 on v3

--- a/solution.py
+++ b/solution.py
@@ -9,9 +9,6 @@
 
 epsilon = 1e-05
 MESH = pl.DeviceIdType.MESH
-K_PIECES = 8
-X_PIECES = 4
-DEPTH = 4
 F32 = jnp.float32
 BF16 = jnp.bfloat16
 N_SEMS = 128
@@ -36,6 +33,7 @@
     x_all,
     x_far,
     x_relay,
+    zeros,
     c_own,
     part_send,
     part_recv,
@@ -124,18 +122,6 @@
         for copy in copies:
             copy.wait()
 
-    y_queue = []
-    y_started = []
-    sent = []
-
-    def pump(count=1):
-        for _ in range(count):
-            if len(y_started) >= DEPTH:
-                for copy in y_started[-DEPTH]:
-                    copy.wait_send()
-                    sent.append(copy)
-            y_started.append(start(y_queue.pop(0)))
-
     def cut(pieces, size):
         return [pl.ds(i * (size // pieces), size // pieces) for i in range(pieces)]
 
@@ -168,7 +154,7 @@
         [
             remote(ref.at[0], g_all.at[m, :, my_keys], device)
             for m, ref in enumerate((gd_ref, gu_ref))
-            for device in y_peers
+            for device in (y_peers[0], y_peers[2])
         ]
     )
     pl.when(h == 1)(lambda: signal(ack.at[0], others))
@@ -208,6 +194,14 @@
             total = total + buffer[i]
         return jnp.concatenate([total[i : i + 1] for i in range(groups)], axis=1)
 
+    copies_zero = [pltpu.make_async_copy(zeros, ref.at[0], lsem.at[14 + m]) for m, ref in enumerate((down_ref, up_ref))]
+    for m, at_end in enumerate((s == n_sections - 1, s == 0)):
+
+        @pl.when(at_end)
+        def _():
+            zeros[...] = jnp.zeros_like(zeros)
+            copies_zero[m].start()
+
     pl.when(low_half)(lambda: pl.semaphore_wait(ack.at[0], 4))
     pl.when(low_relay)(lambda: pl.semaphore_wait(ack.at[3], 2))
     row_halves = cut(2, tok)
@@ -231,19 +225,29 @@
             lanes[m, rows] = fold(values * values)
 
     square_sends = share(squares, jnp.concatenate([to_row(0), to_row(1)], axis=1))
-    w_chunks = {(m, i): w_sends(m, i) for i in range(2) for m in range(2)}
+    w_chunks = {(0, 0): w_sends(0, 0)}
     far_rows = [x_all.at[(h, 1 - h)[i], pl.ds(tok + rows.start, rows.size)] for i, rows in enumerate(row_halves)]
     x_mirror = [remote_cut(2, x_relay.at[row_halves[i]], far_rows[i], across) for i in range(2)]
     pl.when(low_mirror)(lambda: pl.semaphore_wait(ack.at[1], 2))
+    wait(copies_g)
+    wait_recv(g_sends)
+    g_passed = []
+    for m in range(2):
+        for i, step in enumerate((1, 3)):
+            columns = pl.ds(pl.multiple_of(lax.rem(y + step, 4) * keys, keys), keys)
+            block = g_all.at[m, row_halves[i], columns]
+            g_passed.append(remote(block, block, y_peers[2 - 2 * i]))
+    start(g_passed)
+    for m, i in ((1, 0), (0, 1), (1, 1)):
+        w_chunks[m, i] = w_sends(m, i)
     for i in range(2):
         x_turned[1][i].wait_recv()
         x_mirror[1][i].start()
 
     wait_recv(x_turned[0])
-    x_near = start(remote_cut(X_PIECES, xd_ref.at[0], own_x, pair))
-
-    wait(copies_g)
-    wait_recv(g_sends)
+    x_near = start([remote(xd_ref.at[0], own_x, pair)])
+
+    wait_recv(g_passed)
 
     def partial(m, i, use):
         copies_w[i][m].wait()
@@ -273,9 +277,9 @@
 
         if m == 1:
             wait_recv(x_mirror[1])
-            x_pair = [start(remote_cut(2, far_rows[1], far_rows[1], pair))]
+            x_pair = start([remote(far_rows[1], far_rows[1], pair)])
         partial(m, 0, keep)
-        part_sends.append(start(remote_cut(X_PIECES, part_send.at[m], part_recv.at[m], pair)))
+        part_sends.append(start([remote(part_send.at[m], part_recv.at[m], pair)]))
         if m == 0:
             start(x_mirror[0])
             g_far = start([remote(g_scaled.at[1], g_scaled.at[2], mirrored)])
@@ -293,27 +297,25 @@
         wait_recv(part_sends[m])
         partial(m, 1, finish)
 
-    def key_half(half):
-        @pl.loop(0, width // tile)
+    key_sends = []
+    key_own = []
+
+    def key_quarter(half, part):
+        size = width // 2
+
+        @pl.loop(0, size // tile)
         def _(j):
-            columns = pl.ds(pl.multiple_of(j * tile, tile), tile)
+            columns = pl.ds(pl.multiple_of(part * size + j * tile, tile), tile)
             value = jnp.dot(g_scaled[0], x_all[half, :tok, columns], preferred_element_type=F32)
             value += jnp.dot(g_scaled[2], x_all[half, tok:, columns], preferred_element_type=F32)
             key_send[half, :, columns] = value.astype(BF16)
 
-    key_sends = []
-    key_own = []
-
-    def key_out(half):
-        place = wg_ref.at[0, :, w_columns(y, half)]
-        for rows in cut(K_PIECES, keys):
-            group = []
-            for k in range(3):
-                mine = pl.ds(pl.multiple_of(lax.rem(y + k + 1, 4) * keys + rows.start, rows.size), rows.size)
-                group.append(remote(key_send.at[half, mine], place.at[rows], y_peers[k]))
-            y_queue.append(group)
-            key_sends.extend(group)
-        key_own.append(local(key_send.at[half, my_keys], place))
+        columns = pl.ds(part * size, size)
+        place = wg_ref.at[0, :, pl.ds(pl.multiple_of((y * 2 + half) * width + part * size, size), size)]
+        for k in range(3):
+            rows = pl.ds(pl.multiple_of(lax.rem(y + k + 1, 4) * keys, keys), keys)
+            key_sends.extend(start([remote(key_send.at[half, rows, columns], place, y_peers[k])]))
+        key_own.append(local(key_send.at[half, my_keys, columns], place))
 
     def to_column(row):
         return jnp.transpose(jnp.broadcast_to(row, (128, row.shape[1])))
@@ -339,41 +341,51 @@
             value = c_own[m, rows].astype(F32) + (
                 hidden[m, rows] * lanes[0, rows, :1] - x_rows * lanes[1, rows, :1]
             )
-            result[m, rows] = jnp.where(kept[m], value, 0.0).astype(BF16)
+            result[m, rows] = value.astype(BF16)
 
         if m == 1:
             pl.when(s < n_sections - 1)(lambda: pl.semaphore_wait(ack.at[2], 1))
-        shift_sends.extend(start([remote(result.at[m], outs[m].at[0], (behind, ahead)[m])]))
+        copy = remote(result.at[m], outs[m].at[0], (behind, ahead)[m])
+        pl.when(kept[m])(copy.start)
+        shift_sends.append(copy)
 
     own_half(0)
     dot_sends = [share(dots.at[0], to_row(0))]
     wait_recv(x_mirror[0])
-    x_pair.append(start(remote_cut(2, far_rows[0], far_rows[0], pair)))
+    for part in range(2):
+        block = far_rows[0].at[:, pl.ds(part * (width // 2), width // 2)]
+        x_pair += start([remote(block, block, pair)])
     wait_recv(g_far)
-    wait_recv(x_pair[0])
-    key_half(h)
-    key_out(h)
-    pump(DEPTH)
+    x_pair[0].wait_recv()
+    key_quarter(h, 0)
+    key_quarter(h, 1)
     own_half(1)
     dot_sends.append(share(dots.at[1], to_row(1)))
-    pump(2)
     finish_rows(0)
-    pump(2)
     wait_recv(x_near)
-    wait_recv(x_pair[1])
-    key_half(1 - h)
-    key_out(1 - h)
-    pump(2)
+    for part in range(2):
+        x_pair[1 + part].wait_recv()
+        key_quarter(1 - h, part)
     finish_rows(1)
-    pump(len(y_queue))
-    wait_recv(shift_sends)
+
+    for group in [g_sends, g_passed, x_near, *x_turned, *x_mirror, x_pair, square_sends, *part_sends, g_far, *dot_sends]:
+        for copy in group:
+            copy.wait_send()
+    for group in w_chunks.values():
+        for copy in group:
+            copy.wait_send()
+    for m in range(2):
+        pl.when(kept[1 - m])(shift_sends[m].wait_recv)
+        pl.when(kept[m])(shift_sends[m].wait_send)
+
+        @pl.when(jnp.logical_not(kept[1 - m]))
+        def _():
+            copies_zero[m].wait()
+
     wait_recv(key_sends)
     wait(key_own)
-    groups = [g_sends, x_near, *x_turned, *x_mirror, *x_pair, square_sends, *part_sends, g_far, key_sends, *dot_sends, shift_sends, *w_chunks.values()]
-    for group in groups:
-        for copy in group:
-            if not any(copy is other for other in sent):
-                copy.wait_send()
+    for copy in key_sends:
+        copy.wait_send()
 
 
 def place(values):
@@ -420,6 +432,7 @@
             vmem((2, 2 * tok, width), BF16),
             vmem((tok, width), BF16),
             vmem((tok, width), BF16),
+            vmem((tok, width), BF16),
             vmem((2, tok, width), BF16),
             vmem((2, tok, width), BF16),
             vmem((2, tok, width), BF16),

time: 93 us -> 88.1 us (0.947)
  the two profiles are of different devices: /device:TPU:224 before, /device:TPU:1 now
where the time goes in v4:
time: 88.1 us; the launch traced here: 86.4 us
  Pallas kernels  85.8 us (97%)
    pallas_call x1, Pallas kernels, per_device(): pl.pallas_call(functools.partial(kernel, n_sections), out_shape=(jax.Shap...  84.1 us

profile of v4, /device:TPU:1, one launch (start us, length us, event | category | flops | bytes accessed | tf_op | source)
XLA Modules:
  0.0 86.4 jit_solution(1229707566635521849)
XLA Ops:
  0.6 84.1 %relay_backward.1 = (bf16[1,128,8192]{2,1,0:T(8,128)(2,1)S(1)}, bf16[1,256,1024]{2,1,0:T(8,128)(2,1)S(1)}, bf16[1,256,1024]{2,1,0:T(8,128)(2,1)S(1)}) custom-call(bf16[1,128,8192]{2,1,0:T(8,128)(2,1)} %w_ref.1, bf16[1,128,8192]{2,1,0:T(8,128)(2,1)} %mw_ref.1, bf16[1,256,1024]{2,1,0:T(8,128)(2,1)} %xd_ref.1, bf16[1,256,1024]{2,1,0:T(8,128)(2,1)} %cd_ref.1, ...), custom_call_target="tpu_custom_call" | custom-call | tf_op jit(solution)/shard_map/relay_backward/pallas_call | solution.py:419
  84.8 1.7 %place.1 = (bf16[1,128,8192]{2,1,0:T(8,128)(2,1)}, bf16[1,256,1024]{2,1,0:T(8,128)(2,1)}, bf16[1,256,1024]{2,1,0:T(8,128)(2,1)}) custom-call(bf16[1,128,8192]{2,1,0:T(8,128)(2,1)S(1)} %get-tuple-element.6.refs_0_, bf16[1,256,1024]{2,1,0:T(8,128)(2,1)S(1)} %get-tuple-element.7.refs_1_, bf16[1,256,1024]{2,1,0:T(8,128)(2,1)S(1)} %get-tuple-element.8.refs_2_), custom_call_target="tpu_custom_call" | custom-call | tf_op jit(solution)/shard_map/place/pallas_call | solution.py:400

commit v5 on v4

--- a/solution.py
+++ b/solution.py
@@ -11,7 +11,7 @@
 MESH = pl.DeviceIdType.MESH
 F32 = jnp.float32
 BF16 = jnp.bfloat16
-N_SEMS = 128
+N_SEMS = 70
 
 
 def kernel(
@@ -63,6 +63,8 @@
     mirror = n_sections - 1 - s
     mirrored = (mirror, t)
     z = s // 4
+    z_quarter = lax.rem(z, n_sections // 8)
+    at_turn = jnp.logical_or(z_quarter == 0, z_quarter == n_sections // 8 - 1)
     turned = 8 * z + 3 - s
     relays = [(turned, t), (turned, t + 1 - 2 * h)]
     across_s = n_sections - 4 - 8 * z + s
@@ -243,9 +245,10 @@
     for i in range(2):
         x_turned[1][i].wait_recv()
         x_mirror[1][i].start()
-
-    wait_recv(x_turned[0])
-    x_near = start([remote(xd_ref.at[0], own_x, pair)])
+        if i == 0:
+            x_turned[0][0].wait_recv()
+            x_near = start([remote(xd_ref.at[0], own_x, pair)])
+    x_turned[0][1].wait_recv()
 
     wait_recv(g_passed)
 
@@ -281,8 +284,10 @@
         partial(m, 0, keep)
         part_sends.append(start([remote(part_send.at[m], part_recv.at[m], pair)]))
         if m == 0:
-            start(x_mirror[0])
+            pl.when(at_turn)(lambda: [None, start(x_mirror[0])][0])
             g_far = start([remote(g_scaled.at[1], g_scaled.at[2], mirrored)])
+    pl.when(jnp.logical_not(at_turn))(lambda: [None, start(x_mirror[0])][0])
+
     def own_half(m):
         def finish(columns, value):
             if m == 0:

time: 88.1 us -> 85.7 us (0.973); the launches traced: 86.4 us -> 85.7 us
  no operation moved by 1% of the time
where the time goes in v5:
time: 85.7 us
  Pallas kernels  85 us (99%)
    pallas_call x1, Pallas kernels, per_device(): pl.pallas_call(functools.partial(kernel, n_sections), out_shape=(jax.Shap...  83.3 us

profile of v5, /device:TPU:1, one launch (start us, length us, event | category | flops | bytes accessed | tf_op | source)
XLA Modules:
  0.0 85.7 jit_solution(12526115937524520498)
XLA Ops:
  0.6 83.3 %relay_backward.1 = (bf16[1,128,8192]{2,1,0:T(8,128)(2,1)S(1)}, bf16[1,256,1024]{2,1,0:T(8,128)(2,1)S(1)}, bf16[1,256,1024]{2,1,0:T(8,128)(2,1)S(1)}) custom-call(bf16[1,128,8192]{2,1,0:T(8,128)(2,1)} %w_ref.1, bf16[1,128,8192]{2,1,0:T(8,128)(2,1)} %mw_ref.1, bf16[1,256,1024]{2,1,0:T(8,128)(2,1)} %xd_ref.1, bf16[1,256,1024]{2,1,0:T(8,128)(2,1)} %cd_ref.1, ...), custom_call_target="tpu_custom_call" | custom-call | tf_op jit(solution)/shard_map/relay_backward/pallas_call | solution.py:424
  84.0 1.7 %place.1 = (bf16[1,128,8192]{2,1,0:T(8,128)(2,1)}, bf16[1,256,1024]{2,1,0:T(8,128)(2,1)}, bf16[1,256,1024]{2,1,0:T(8,128)(2,1)}) custom-call(bf16[1,128,8192]{2,1,0:T(8,128)(2,1)S(1)} %get-tuple-element.6.refs_0_, bf16[1,256,1024]{2,1,0:T(8,128)(2,1)S(1)} %get-tuple-element.7.refs_1_, bf16[1,256,1024]{2,1,0:T(8,128)(2,1)S(1)} %get-tuple-element.8.refs_2_), custom_call_target="tpu_custom_call" | custom-call | tf_op jit(solution)/shard_map/place/pallas_call | solution.py:405

commit v6 on v5

--- a/solution.py
+++ b/solution.py
@@ -272,6 +272,7 @@
         return inv_rms
 
     inv_rms = scale_g()
+    g_far = start([remote(g_scaled.at[1], g_scaled.at[2], mirrored)])
     part_sends = []
     for m in range(2):
 
@@ -285,7 +286,6 @@
         part_sends.append(start([remote(part_send.at[m], part_recv.at[m], pair)]))
         if m == 0:
             pl.when(at_turn)(lambda: [None, start(x_mirror[0])][0])
-            g_far = start([remote(g_scaled.at[1], g_scaled.at[2], mirrored)])
     pl.when(jnp.logical_not(at_turn))(lambda: [None, start(x_mirror[0])][0])
 
     def own_half(m):
@@ -357,13 +357,13 @@
     own_half(0)
     dot_sends = [share(dots.at[0], to_row(0))]
     wait_recv(x_mirror[0])
-    for part in range(2):
-        block = far_rows[0].at[:, pl.ds(part * (width // 2), width // 2)]
-        x_pair += start([remote(block, block, pair)])
     wait_recv(g_far)
     x_pair[0].wait_recv()
     key_quarter(h, 0)
     key_quarter(h, 1)
+    for part in range(2):
+        block = far_rows[0].at[:, pl.ds(part * (width // 2), width // 2)]
+        x_pair += start([remote(block, block, pair)])
     own_half(1)
     dot_sends.append(share(dots.at[1], to_row(1)))
     finish_rows(0)

time: 85.7 us -> 84.3 us (0.984)
  Pallas kernels: 85 us -> 83 us
    pallas_call x1, Pallas kernels: 83.3 us -> 81.3 us  [per_device(): pl.pallas_call(functools.partial(kernel, n_sections), out_shape=(jax.Shap...]
where the time goes in v6:
time: 84.3 us; the launch traced here: 83.6 us
  Pallas kernels  83 us (98%)
    pallas_call x1, Pallas kernels, per_device(): pl.pallas_call(functools.partial(kernel, n_sections), out_shape=(jax.Shap...  81.3 us

profile of v6, /device:TPU:1, one launch (start us, length us, event | category | flops | bytes accessed | tf_op | source)
XLA Modules:
  0.0 83.6 jit_solution(14984661704344311684)
XLA Ops:
  0.6 81.3 %relay_backward.1 = (bf16[1,128,8192]{2,1,0:T(8,128)(2,1)S(1)}, bf16[1,256,1024]{2,1,0:T(8,128)(2,1)S(1)}, bf16[1,256,1024]{2,1,0:T(8,128)(2,1)S(1)}) custom-call(bf16[1,128,8192]{2,1,0:T(8,128)(2,1)} %w_ref.1, bf16[1,128,8192]{2,1,0:T(8,128)(2,1)} %mw_ref.1, bf16[1,256,1024]{2,1,0:T(8,128)(2,1)} %xd_ref.1, bf16[1,256,1024]{2,1,0:T(8,128)(2,1)} %cd_ref.1, ...), custom_call_target="tpu_custom_call" | custom-call | tf_op jit(solution)/shard_map/relay_backward/pallas_call | solution.py:424
  81.9 1.7 %place.1 = (bf16[1,128,8192]{2,1,0:T(8,128)(2,1)}, bf16[1,256,1024]{2,1,0:T(8,128)(2,1)}, bf16[1,256,1024]{2,1,0:T(8,128)(2,1)}) custom-call(bf16[1,128,8192]{2,1,0:T(8,128)(2,1)S(1)} %get-tuple-element.6.refs_0_, bf16[1,256,1024]{2,1,0:T(8,128)(2,1)S(1)} %get-tuple-element.7.refs_1_, bf16[1,256,1024]{2,1,0:T(8,128)(2,1)S(1)} %get-tuple-element.8.refs_2_), custom_call_target="tpu_custom_call" | custom-call | tf_op jit(solution)/shard_map/place/pallas_call | solution.py:405
